TPU v7x, 256 devices: a whole 4x4x8 slice. The times are simulated.
256 devices in a mesh: group: 8 (over x, core), local: 32 (over z, y).
Axes of the slice: x: 4, y: 4, z: 8, core: 2. Of those that a mesh axis runs over, the one named last changes fastest.
Arguments:
- coords: float32 [3, 262144], P(None, ('group', 'local')), may hold values from -6 to 6
- inv_length: float32 [3], replicated, may hold values from 0.5 to 2
- noise: float32 [262144], P(('group', 'local')), may hold values from 1 to 4
- order: int32 [256, 1024], P(('group', 'local')), may hold values from 0 to 1023, each once within a row
- basis: bfloat16 [262144, 8, 256], P(('group', 'local')), may hold values from -6 to 6
- probes: float32 [128, 262144], P(None, ('group', 'local')), may hold values from -8 to 8
Outputs:
- solution: float32 [128, 262144], P(None, ('group', 'local'))
- residual: float32 [128, 262144], P(None, ('group', 'local'))
All inputs are finite; a program needn't handle non-finite values.
Results may differ from a plain program's by a relative error of at most 0.0003.
Values sent between devices are 32-bit elements; how exact they have to be, the bound alone decides.
No kernel may reach another device: no remote copies, remote signals or barrier semaphores. Data moves between devices by JAX's collectives and lax.ppermute only.
A program may use at most 64 MiB of HBM per device.

v0:
```python
import functools
import math

import jax
import jax.numpy as jnp
from jax import lax
from jax.experimental import pallas as pl
from jax.experimental.pallas import tpu as pltpu
from jax.sharding import PartitionSpec as P

GAMMA = 0.08
ROOT_OF_THREE = math.sqrt(3.0)
SHIFT = 3.5
LEVELS = 8
RANK = 256
LEAF = 1024
PROBES = 128
PART = PROBES // 4
ROWS = PART // 2
LANES = 128
CHUNKS = 4
START_LIMIT = 52
F32 = jnp.float32
BF16 = jnp.bfloat16
VMEM = pl.BlockSpec(memory_space=pltpu.VMEM)
SMEM = pl.BlockSpec(memory_space=pltpu.SMEM)
ANY = pl.BlockSpec(memory_space=pl.ANY)
HBM = pl.BlockSpec(memory_space=pltpu.HBM)


def factor(level):
    return GAMMA / (LEAF * 2.0**level)


def call(kernel, out_shape, *args, scratch=(), smem=0, anywhere=0, outside=0, flops=0, limit=16, outs=None):
    held = len(args) - smem - anywhere - outside
    return pl.pallas_call(
        kernel,
        out_shape=out_shape,
        in_specs=[SMEM] * smem + [VMEM] * held + [ANY] * anywhere + [HBM] * outside,
        out_specs=outs or jax.tree.map(lambda _: VMEM, out_shape),
        scratch_shapes=list(scratch),
        compiler_params=pltpu.CompilerParams(vmem_limit_bytes=limit * 2**20),
        cost_estimate=pl.CostEstimate(
            flops=flops, bytes_accessed=2**20, transcendentals=0
        ),
    )(*args)


def shape(*dims, dtype=F32):
    return jax.ShapeDtypeStruct(dims, dtype)


def dot(a, b):
    return jnp.dot(a, b, preferred_element_type=F32)


def dot_t(a, b):
    return lax.dot_general(a, b, (((1,), (1,)), ((), ())), preferred_element_type=F32)


def split(x):
    high = x.astype(BF16)
    return high, (x - high.astype(F32)).astype(BF16)


def level_lanes(i):
    return slice(i * RANK, (i + 1) * RANK)


def owned(i, core):
    return pl.ds(pl.multiple_of(i * PART + core * ROWS, ROWS), ROWS)


def quarter(y, k):
    return pl.ds(pl.multiple_of((y ^ k) * PART, PART), PART)


def coefficients(v, basis_ref, levels, full_ref):
    for i, level in enumerate(levels):
        full_ref[:, level_lanes(i)] = dot(v, basis_ref[level])


def own_half(core):
    return pl.ds(pl.multiple_of(core * LANES, LANES), LANES)


def scatter_halves(core, full_ref, send_ref, keep_ref, at):
    for i in range(2):
        lanes = slice(i * LANES, (i + 1) * LANES)
        half = full_ref.at[:, level_lanes(i)]
        keep_ref[:, lanes] = half[:, own_half(core)]
        send_ref[:, at + i * LANES : at + (i + 1) * LANES] = half[:, own_half(1 - core)]


def start_kernel(core_ref, v_hbm, flat_ref, basis_out, send_ref, keep_ref, low_ref, full, held, basis_ref, v_ref, sems):
    rows = LEAF * LEVELS // CHUNKS
    points = LEAF // CHUNKS
    copies = [
        pltpu.make_async_copy(
            flat_ref.at[pl.ds(i * rows, rows)], held.at[pl.ds(i * rows, rows)], sems.at[i]
        )
        for i in range(CHUNKS)
    ]
    saves = [
        pltpu.make_async_copy(
            basis_ref.at[:, pl.ds(i * points, points)],
            basis_out.at[:, pl.ds(i * points, points)],
            sems.at[CHUNKS + 1 + i],
        )
        for i in range(CHUNKS)
    ]
    last = pltpu.make_async_copy(v_hbm, v_ref, sems.at[CHUNKS])
    for copy in copies:
        copy.start()
    last.start()
    width = 32
    block = width * LEVELS
    to = lax.broadcasted_iota(jnp.int32, (block, block), 0)
    at = lax.broadcasted_iota(jnp.int32, (block, block), 1)
    source = (to & (width - 1)) * LEVELS + (to >> 5)
    order = jnp.where(at == source, 1.0, 0.0).astype(BF16)
    for i, copy in enumerate(copies):
        copy.wait()
        for j in range(i * rows // block, (i + 1) * rows // block):
            moved = dot(order, held[j * block : (j + 1) * block, :]).astype(BF16)
            for level in range(LEVELS):
                basis_ref[level, j * width : (j + 1) * width, :] = moved[
                    level * width : (level + 1) * width
                ]
        saves[i].start()
    last.wait()
    v = v_ref[...].astype(BF16)
    send_ref[:, :RANK] = dot(v, basis_ref[5])
    coefficients(v, basis_ref, (6, 7), full)
    scatter_halves(core_ref[0], full, send_ref, keep_ref, RANK)
    coefficients(v, basis_ref, (2, 3, 4), low_ref)
    for save in saves:
        save.wait()


def whole_kernel(levels, v_ref, basis_ref, gate_ref, out_ref):
    coefficients(v_ref[...].astype(BF16), basis_ref, levels, out_ref)


def parts_kernel(y_ref, low_ref, keep_ref, other_ref, *parts):
    for k, part in enumerate(parts):
        at = quarter(y_ref[0], k)
        part[:, : 3 * RANK] = low_ref[at, :]
        part[:, 3 * RANK : 4 * RANK] = other_ref[at, :RANK]
        part[:, 4 * RANK :] = keep_ref[at, :] + other_ref[at, RANK:]


def gather_kernel(order_ref, values_ref, gate_ref, out_ref):
    x = values_ref[...]
    a, rest = x.astype(BF16), x - x.astype(BF16).astype(F32)
    b, c = split(rest)
    pieces = jnp.concatenate([a, b, c], axis=0)
    step = 256
    total = None
    for i in range(LEAF // step):
        source = lax.broadcasted_iota(jnp.int32, (step, LEAF), 0) + i * step
        hot = jnp.where(source == order_ref[...], 1.0, 0.0).astype(BF16)
        term = dot(pieces[:, i * step : (i + 1) * step], hot)
        total = term if total is None else total + term
    out_ref[...] = total[:8] + total[8:16] + total[16:]


def matrix_kernel(half, values_ref, high_ref, low_ref):
    step = 128
    columns = values_ref[...].T
    for i in range(LEAF // 2 // step):
        at = slice(half * LEAF // 2 + i * step, half * LEAF // 2 + (i + 1) * step)
        square = None
        for c in range(3):
            diff = columns[at, c : c + 1] - values_ref[c : c + 1, :]
            square = diff * diff if square is None else square + diff * diff
        t = ROOT_OF_THREE * jnp.sqrt(square)
        high, low = split((1.0 + t) * jnp.exp(-t))
        high_ref[i * step : (i + 1) * step, :] = high
        low_ref[i * step : (i + 1) * step, :] = low


def near_kernel(v_ref, values_ref, high0, high1, low0, low1, *rest):
    out_ref = rest[-1]
    v = v_ref[...]
    v_high, v_low = split(v)
    both = LEAF // 2
    first, second = slice(0, both), slice(both, LEAF)
    out_ref[...] = (
        (dot(v_low[:, first], high0[...]) + dot(v_low[:, second], high1[...]))
        + (dot(v_high[:, first], low0[...]) + dot(v_high[:, second], low1[...]))
        + (dot(v_high[:, first], high0[...]) + dot(v_high[:, second], high1[...]))
        + values_ref[3:4, :] * v
    )


def base_kernel(near_ref, v_ref, basis_ref, sib0, sib1, out_ref):
    zero = (sib0[:, :RANK] * factor(0)).astype(BF16)
    one = (sib1[...] * factor(1)).astype(BF16)
    out_ref[...] = (
        (near_ref[...] - SHIFT * v_ref[...])
        + dot_t(zero, basis_ref[0])
        + dot_t(one, basis_ref[1])
    )


def far_first_kernel(y_ref, basis_ref, b0, b1, b2, b3, out_ref, held):
    for k, back in enumerate((b0, b1, b2, b3)):
        for i in range(4):
            held[quarter(y_ref[0], k), level_lanes(i)] = (
                back[:, level_lanes(i)] * factor(2 + i)
            ).astype(BF16)
    total = None
    for i in range(4):
        term = dot_t(held[:, level_lanes(i)], basis_ref[2 + i])
        total = term if total is None else total + term
    out_ref[...] = total


def far_of_halves(core, own_ref, other_ref, levels, basis_ref, held, total):
    for i in range(len(levels)):
        for ref, side in ((own_ref, core), (other_ref, 1 - core)):
            scaled = (ref[:, level_lanes(i)] * factor(levels[i])).astype(BF16)
            for j in range(4):
                held[owned(j, side), level_lanes(i)] = scaled[j * ROWS : (j + 1) * ROWS]
    for i, level in enumerate(levels):
        total += dot_t(held[:, level_lanes(i)], basis_ref[level])
    return total


def far_second_kernel(core_ref, near_ref, basis_ref, own_ref, other_ref, out_ref, held):
    out_ref[...] = far_of_halves(
        core_ref[0], own_ref, other_ref, (0, 1, 2), basis_ref, held, near_ref[...]
    )


def far_high(core, own_ref, other_ref, basis_ref, held):
    for i in range(2):
        lanes = slice(i * LANES, (i + 1) * LANES)
        half = held.at[:, level_lanes(i)]
        half[:, own_half(core)] = (own_ref[:, lanes] * factor(6 + i)).astype(BF16)
        half[:, own_half(1 - core)] = (other_ref[:, lanes] * factor(6 + i)).astype(BF16)
    return dot_t(held[:, level_lanes(0)], basis_ref[6]) + dot_t(
        held[:, level_lanes(1)], basis_ref[7]
    )


def give_halves(core, full_ref, send_ref, keep_ref):
    for i in range(4):
        to = slice(i * ROWS, (i + 1) * ROWS)
        send_ref[to, :] = full_ref[owned(i, 1 - core), :]
        keep_ref[to, :] = full_ref[owned(i, core), :]


def middle_kernel(core_ref, own_ref, other_ref, *refs):
    basis_ref, base_ref, low_ref, image_ref, far_ref, send_ref, keep_ref, held, full = refs
    core = core_ref[0]
    far = low_ref[...] + far_high(core, own_ref, other_ref, basis_ref, held)
    far_ref[...] = far
    image = base_ref[...] + far
    image_ref[...] = image
    coefficients(image.astype(BF16), basis_ref, range(LEVELS), full)
    give_halves(core, full, send_ref, keep_ref)


def dots_kernel(core_ref, base_ref, far_ref, image_ref, near_ref, v_ref, values_ref, high0, high1, gate_ref, *refs):
    send_ref, keep_ref, block_ref = refs
    far, near, image, v = far_ref[...], near_ref[...], image_ref[...], v_ref[...]
    rounded = far.astype(BF16)
    half = LEAF // 2
    own = (
        dot(rounded[:, :half], high0[...])
        + dot(rounded[:, half:], high1[...])
        + values_ref[3:4, :] * far
    )
    curve = base_ref[...] * near + far * (2.0 * near + own)
    lane = lax.broadcasted_iota(jnp.int32, (PROBES, LANES), 1)
    block = jnp.zeros((PROBES, LANES), F32)
    for i, term in enumerate((v * v, v * image, image * image, curve)):
        block = jnp.where(lane == i, jnp.sum(term, axis=1, keepdims=True), block)
    block_ref[...] = block
    give_halves(core_ref[0], block_ref, send_ref, keep_ref)


def final_kernel(core_ref, own_ref, other_ref, basis_ref, low_ref, image_ref, v_ref, x_ref, r_ref, held, dots):
    core = core_ref[0]
    for ref, side in ((own_ref, core), (other_ref, 1 - core)):
        for j in range(4):
            dots[owned(j, side), :] = ref[j * ROWS : (j + 1) * ROWS, 5 * RANK :]
    second = far_of_halves(
        core, own_ref, other_ref, (3, 4, 5, 6, 7), basis_ref, held, low_ref[...]
    )
    n0, n1, n2, n3 = (dots[:, i : i + 1] for i in range(4))
    m1 = n1 + SHIFT * n0
    mixed = n2 + SHIFT * n1
    alpha = n0 / m1
    norm = alpha * (alpha * n2 - n1 * (n1 / m1))
    curve = alpha * alpha * (n3 - mixed * (mixed / m1))
    alpha_next = norm / curve
    grown = alpha * (mixed / m1)
    v = v_ref[...]
    shifted = image_ref[...]
    image = shifted + SHIFT * v
    x_ref[...] = alpha * v + alpha_next * (grown * v - alpha * shifted)
    r_ref[...] = (n1 / m1) * v - alpha * shifted - alpha_next * (grown * image - alpha * second)


def assemble_kernel(y_ref, b0, b1, b2, b3, out_ref):
    for k, back in enumerate((b0, b1, b2, b3)):
        out_ref[quarter(y_ref[0], k), :] = back[:, 4 * RANK :]


def pair_dot(a, b, level):
    return 2.0 * factor(level) * jnp.sum(a * b, axis=1, keepdims=True)


def in_lane(i, x):
    lane = lax.broadcasted_iota(jnp.int32, (PART, LANES), 1)
    return jnp.where(lane == i, x, 0.0)


def sum_kernel(r0, r1, r2, r3, gate_ref, total_ref):
    total_ref[...] = (r0[...] + r1[...]) + (r2[...] + r3[...])


def shift_kernel(own, other, out_ref):
    out_ref[...] = own[:, RANK:] + other[:, RANK:]


def six_seven_kernel(own, other, *refs):
    six_ref, seven_ref = refs[-2:]
    six, seven = slice(2 * RANK, 2 * RANK + LANES), slice(2 * RANK + LANES, 3 * RANK)
    six_ref[...] = own[:, six] + other[:, six]
    seven_ref[...] = own[:, seven] + other[:, seven]


def join_first_kernel(two, three, four, own, x1, x2, x3, gate_ref, out_ref):
    out_ref[:, level_lanes(0)] = two[:, :RANK]
    out_ref[:, level_lanes(1)] = three[:, :RANK]
    out_ref[:, level_lanes(2)] = four[:, :RANK]
    out_ref[:, level_lanes(3)] = own[:, level_lanes(1)] + four[:, level_lanes(1)]
    out_ref[:, 4 * RANK : 4 * RANK + LANES] = x1[...]
    out_ref[:, 4 * RANK + LANES :] = x2[...] + x3[...]


def merge_kernel(y_ref, keep_ref, other_ref, keep_dots, other_dots, *parts):
    end = 6 * RANK
    for k, part_ref in enumerate(parts):
        at = pl.ds(pl.multiple_of((y_ref[0] ^ k) * ROWS, ROWS), ROWS)
        for level in range(6):
            part_ref[:, level_lanes(2 * level)] = keep_ref[at, level_lanes(level)]
            part_ref[:, level_lanes(2 * level + 1)] = other_ref[at, level_lanes(level)]
        part_ref[:, 2 * end : -LANES] = keep_ref[at, end:] + other_ref[at, end:]
        part_ref[:, -LANES:] = keep_dots[at, :] + other_dots[at, :]


def add_dot(total_ref, lane, term):
    lanes = lax.broadcasted_iota(jnp.int32, (ROWS, LANES), 1)
    total_ref[:, -LANES:] += jnp.where(lanes == lane, term, 0.0)


def y_dots_kernel(r0, r1, r2, r3, gate_ref, total_ref):
    pair = 2 * RANK
    start = 2 * pair
    total_ref[...] = (r0[:, start:] + r1[:, start:]) + (r2[:, start:] + r3[:, start:])
    a, b = slice(0, pair), slice(pair, start)
    term = pair_dot(r0[:, a], r1[:, a], 0) + pair_dot(r2[:, a], r3[:, a], 0)
    term += pair_dot(r0[:, b] + r1[:, b], r2[:, b] + r3[:, b], 1)
    add_dot(total_ref, 3, term)


def step_kernel(level, own, other, *rest):
    total_ref = rest[-1]
    pair = 2 * RANK
    total_ref[...] = own[:, pair:] + other[:, pair:]
    add_dot(total_ref, 3, pair_dot(own[:, :pair], other[:, :pair], level))


def last_step_kernel(own, other, g1, g2, g3, five_ref, total_ref):
    pair = 2 * RANK
    term = pair_dot(own[:, :pair], other[:, :pair], 4)
    five_ref[...] = own[:, pair : 2 * pair] + other[:, pair : 2 * pair]
    total_ref[...] = own[:, 2 * pair :] + other[:, 2 * pair :]
    term += pair_dot(five_ref[:, level_lanes(0)], five_ref[:, level_lanes(1)], 5)
    add_dot(total_ref, 3, term)


def low_join_kernel(r0, r1, r2, r3, two, gate_ref, *outs):
    r = (r0, r1, r2, r3)
    pair = 2 * RANK
    zero, one = slice(0, pair), slice(pair, 2 * pair)
    for k, out in enumerate(outs):
        out[:, zero] = r[k ^ 1][:, zero]
        out[:, one] = r[k ^ 2][:, one] + r[k ^ 3][:, one]
        out[:, 2 * pair :] = two[:, :pair]


def high_join_kernel(three, four, five, own, x1, x2, x3, out_ref):
    a, b, q = slice(0, RANK), slice(RANK, 2 * RANK), slice(2 * RANK, 2 * RANK + LANES)
    far = x2[:, b] + x3[:, b]
    pair = 2 * RANK
    out_ref[:, :pair] = three[:, :pair]
    out_ref[:, pair : 2 * pair] = four[:, :pair]
    out_ref[:, level_lanes(4)] = five[:, level_lanes(1)]
    out_ref[:, level_lanes(5)] = five[:, level_lanes(0)]
    out_ref[:, level_lanes(6)] = x1[:, a]
    out_ref[:, level_lanes(7)] = far
    out_ref[:, 8 * RANK :] = (own[:, q] + x1[:, q]) + (x2[:, q] + x3[:, q])
    term = pair_dot(own[:, a], x1[:, a], 6) + pair_dot(x2[:, a], x3[:, a], 6)
    term += pair_dot(own[:, b] + x1[:, b], far, 7)
    add_dot(out_ref, 3, term)


def gather_kernel_of(levels, shared, y_ref, b0, b1, b2, b3, *rest):
    own_ref, send_ref = rest[-2:]
    for k, back in enumerate((b0, b1, b2, b3)):
        at = pl.ds(pl.multiple_of((y_ref[0] ^ k) * ROWS, ROWS), ROWS)
        for i in range(levels):
            own_ref[at, level_lanes(i)] = back[:, level_lanes(2 * i)]
            send_ref[at, level_lanes(i)] = back[:, level_lanes(2 * i + 1)]
        if shared:
            own_ref[at, levels * RANK :] = back[:, 2 * levels * RANK :]
            send_ref[at, levels * RANK :] = back[:, 2 * levels * RANK :]


def swap(x, axis, mask):
    return lax.ppermute(x, axis, [(i, i ^ mask) for i in range(lax.axis_size(axis))])


def over_y(x):
    return [x[0]] + [swap(x[k], "local", k) for k in (1, 2, 3)]


Z1, Z2, Z3 = ("local", 4), ("local", 8), ("local", 24)
CORE, X1, X2, X3 = ("group", 1), ("group", 2), ("group", 4), ("group", 6)


def rows(lanes):
    return shape(ROWS, lanes)


def part(lanes):
    return shape(PART, lanes)


def per_device(coords, inv_length, noise, order, basis, probes):
    y = (lax.axis_index("local") & 3).astype(jnp.int32)[None]
    core = (lax.axis_index("group") & 1).astype(jnp.int32)[None]
    flat = basis.reshape(LEAF * LEVELS, RANK)
    square = shape(LEAF // 2, LEAF, dtype=BF16)
    vectors = shape(PROBES, LEAF)
    both = shape(PROBES, RANK)

    basis, send, keep, low = call(
        start_kernel,
        (
            shape(LEVELS, LEAF, RANK, dtype=BF16),
            shape(PROBES, 2 * RANK),
            both,
            shape(PROBES, 3 * RANK),
        ),
        core,
        pltpu.with_memory_space_constraint(probes, pltpu.HBM),
        pltpu.with_memory_space_constraint(flat, pltpu.HBM),
        scratch=[
            pltpu.VMEM((PROBES, 2 * RANK), F32),
            pltpu.VMEM((LEAF * LEVELS, RANK), BF16),
            pltpu.VMEM((LEVELS, LEAF, RANK), BF16),
            pltpu.VMEM((PROBES, LEAF), F32),
            pltpu.SemaphoreType.DMA((2 * CHUNKS + 1,)),
        ],
        smem=1,
        outside=2,
        flops=2**31,
        limit=START_LIMIT,
        outs=(ANY, VMEM, VMEM, VMEM),
    )
    other = swap(send, *CORE)
    parts = call(parts_kernel, (part(5 * RANK),) * 4, y, low, keep, other, smem=1)
    moved = over_y(parts)

    values = jnp.concatenate(
        [coords * inv_length[:, None], noise[None, :], jnp.zeros((4, LEAF), F32)], axis=0
    )
    values = call(
        gather_kernel, shape(8, LEAF), order, values, parts[0], anywhere=1, flops=2**26
    )
    high0, low0 = call(
        functools.partial(matrix_kernel, 0), (square, square), values, flops=2**30
    )
    high1, low1 = call(
        functools.partial(matrix_kernel, 1), (square, square), values, flops=2**30
    )
    matrix = (values, high0, high1, low0, low1)
    near = call(near_kernel, vectors, probes, *matrix, flops=2**30)

    total = call(sum_kernel, part(5 * RANK), *moved, near, anywhere=1)
    two = swap(total, *Z1)
    leaf = call(
        functools.partial(whole_kernel, (0, 1)),
        shape(PROBES, 2 * RANK),
        probes,
        basis,
        total,
        anywhere=1,
        flops=2**28,
    )
    leaf_other = swap(leaf, "local", 1)
    total = call(shift_kernel, part(4 * RANK), total, two)
    three = swap(total, *Z2)
    leaf_next = call(shift_kernel, both, leaf, leaf_other)
    one = swap(leaf_next, "local", 3)
    total = call(shift_kernel, part(3 * RANK), total, three)
    four = swap(total, *Z3)
    six, seven = call(
        six_seven_kernel, (part(LANES),) * 2, total, four, one, anywhere=1
    )
    x1, x2, x3 = swap(six, *X1), swap(seven, *X2), swap(seven, *X3)
    base = call(
        base_kernel, vectors, near, probes, basis, leaf_other, one, flops=2**28
    )
    base_near = call(near_kernel, vectors, base, *matrix, flops=2**30)
    back = call(
        join_first_kernel,
        part(5 * RANK),
        two,
        three,
        four,
        total,
        x1,
        x2,
        x3,
        base_near,
        anywhere=1,
    )
    back = over_y([back] * 4)
    own = call(assemble_kernel, both, y, *back, smem=1)
    other = swap(own, *CORE)
    far = call(
        far_first_kernel,
        vectors,
        y,
        basis,
        *back,
        scratch=[pltpu.VMEM((PROBES, 4 * RANK), BF16)],
        smem=1,
        flops=2**29,
    )
    wide, half = LEVELS * RANK, PROBES // 2
    image, far, send, keep = call(
        middle_kernel,
        (vectors, vectors, shape(half, wide), shape(half, wide)),
        core,
        own,
        other,
        basis,
        base,
        far,
        scratch=[pltpu.VMEM((PROBES, 2 * RANK), BF16), pltpu.VMEM((PROBES, wide), F32)],
        smem=1,
        flops=2**30,
    )
    other = swap(send, *CORE)
    send, keep_dots = call(
        dots_kernel,
        (shape(half, LANES), shape(half, LANES)),
        core,
        base,
        far,
        image,
        base_near,
        probes,
        values,
        high0,
        high1,
        send,
        scratch=[pltpu.VMEM((PROBES, LANES), F32)],
        smem=1,
        anywhere=1,
        flops=2**28,
    )
    other_dots = swap(send, *CORE)
    parts = call(
        merge_kernel,
        (rows(14 * RANK + LANES),) * 4,
        y,
        keep,
        other,
        keep_dots,
        other_dots,
        smem=1,
    )
    moved = over_y(parts)
    near = call(
        near_kernel, vectors, image, *matrix, parts[0], anywhere=1, flops=2**30
    )
    total = call(
        y_dots_kernel, rows(10 * RANK + LANES), *moved, near, anywhere=1
    )
    two = swap(total, *Z1)
    total = call(functools.partial(step_kernel, 2), rows(8 * RANK + LANES), total, two)
    three = swap(total, *Z2)
    back = call(low_join_kernel, (rows(6 * RANK),) * 4, *moved, two, total, anywhere=1)
    back = over_y(back)
    total = call(functools.partial(step_kernel, 3), rows(6 * RANK + LANES), total, three)
    four = swap(total, *Z3)
    five, total = call(
        last_step_kernel,
        (rows(2 * RANK), rows(2 * RANK + LANES)),
        total,
        four,
        *back[1:],
        anywhere=3,
    )
    x1, x2, x3 = swap(total, *X1), swap(total, *X2), swap(total, *X3)
    low_own, send = call(
        functools.partial(gather_kernel_of, 3, False),
        (shape(PROBES // 2, 3 * RANK),) * 2,
        y,
        *back,
        smem=1,
    )
    low_other = swap(send, *CORE)
    high_back = call(
        high_join_kernel, rows(8 * RANK + LANES), three, four, five, total, x1, x2, x3
    )
    high_back = over_y([high_back] * 4)
    partial_second = call(
        far_second_kernel,
        vectors,
        core,
        near,
        basis,
        low_own,
        low_other,
        scratch=[pltpu.VMEM((PROBES, 3 * RANK), BF16)],
        smem=1,
        flops=2**29,
    )
    own, send = call(
        functools.partial(gather_kernel_of, 3, True),
        (shape(PROBES // 2, 5 * RANK + LANES),) * 2,
        y,
        *high_back,
        partial_second,
        smem=1,
        anywhere=1,
    )
    other = swap(send, *CORE)
    return call(
        final_kernel,
        (vectors, vectors),
        core,
        own,
        other,
        basis,
        partial_second,
        image,
        probes,
        scratch=[pltpu.VMEM((PROBES, 5 * RANK), BF16), pltpu.VMEM((PROBES, LANES), F32)],
        smem=1,
        flops=2**29,
    )


def solution(mesh):
    in_specs = (
        P(None, ("group", "local")),
        P(),
        P(("group", "local")),
        P(("group", "local"), None),
        P(("group", "local"), None, None),
        P(None, ("group", "local")),
    )
    out_specs = (P(None, ("group", "local")), P(None, ("group", "local")))
    return jax.shard_map(
        per_device, mesh=mesh, in_specs=in_specs, out_specs=out_specs, check_vma=False
    )
```

profile of v0, /device:TPU:1, one launch (start us, length us, event | category | flops | bytes accessed | tf_op | source)
XLA Modules:
  0.0 123.6 jit_solution(9528946166922672098)
XLA Ops:
  0.7 4.1 %shard_map.77 = (bf16[8,1024,256]{2,1,0:T(8,128)(2,1)}, f32[128,512]{1,0:T(8,128)S(1)}, f32[128,256]{1,0:T(8,128)S(1)}, f32[128,768]{1,0:T(8,128)S(1)}) custom-call(s32[1]{0:T(128)} %bitcast.core_ref, f32[128,1024]{1,0:T(8,128)} %v_ref.9, bf16[8192,256]{1,0:T(8,128)(2,1)} %bitcast.5), custom_call_target="tpu_custom_call" | custom-call | flops 2147483648 | bytes 1048576 | tf_op jit(solution)/shard_map/pallas_call | solution.py:37
  4.8 3.3 %collective-permute-start = (f32[128,512]{1,0:T(8,128)S(1)}, f32[128,512]{1,0:T(8,128)S(1)}, u32[]{:S(2)}, u32[]{:S(2)}) collective-permute-start(f32[128,512]{1,0:T(8,128)S(1)} %get-tuple-element.38), channel_id=1, source_target_pairs={{0,32},{32,0},{64,96},{96,64},{128,160},{160,128},{192,224},{224,1... | collective-permute-start | bytes 786440 | tf_op jit(solution)/shard_map/ppermute | solution.py:428
  9.4 2.2 %collective-permute-start.2 = (f32[32,1280]{1,0:T(8,128)S(1)}, f32[32,1280]{1,0:T(8,128)S(1)}, u32[]{:S(2)}, u32[]{:S(2)}) collective-permute-start(f32[32,1280]{1,0:T(8,128)S(1)} %get-tuple-element.41), channel_id=1, source_target_pairs={{0,2},{1,3},{2,0},{3,1},{4,6},{5,7},{6,4},{7,5},{8,10},{9,11},{10,... | collective-permute-start | bytes 491528 | tf_op jit(solution)/shard_map/ppermute | solution.py:428
  19.1 2.7 %collective-permute-done.3.r3 = f32[32,1280]{1,0:T(8,128)S(1)} collective-permute-done((f32[32,1280]{1,0:T(8,128)S(1)}, f32[32,1280]{1,0:T(8,128)S(1)}, u32[]{:S(2)}, u32[]{:S(2)}) %collective-permute-start.3) | collective-permute-done | bytes 163872 | tf_op jit(solution)/shard_map/ppermute | solution.py:428
  24.0 2.8 %collective-permute-done.4.other.two = f32[32,1280]{1,0:T(8,128)S(1)} collective-permute-done((f32[32,1280]{1,0:T(8,128)S(1)}, f32[32,1280]{1,0:T(8,128)S(1)}, u32[]{:S(2)}, u32[]{:S(2)}) %collective-permute-start.4) | collective-permute-done | bytes 163872 | tf_op jit(solution)/shard_map/ppermute | solution.py:428
  26.8 3.1 %collective-permute-start.5 = (f32[32,1024]{1,0:T(8,128)S(1)}, f32[32,1024]{1,0:T(8,128)S(1)}, u32[]{:S(2)}, u32[]{:S(2)}) collective-permute-start(f32[32,1024]{1,0:T(8,128)S(1)} %shard_map.84.own), channel_id=1, source_target_pairs={{0,8},{1,9},{2,10},{3,11},{4,12},{5,13},{6,14},{7,15},{8,0},{9,1},... | collective-permute-start | bytes 393224 | tf_op jit(solution)/shard_map/ppermute | solution.py:428
  30.5 3.6 %collective-permute-done.5.other.three = f32[32,1024]{1,0:T(8,128)S(1)} collective-permute-done((f32[32,1024]{1,0:T(8,128)S(1)}, f32[32,1024]{1,0:T(8,128)S(1)}, u32[]{:S(2)}, u32[]{:S(2)}) %collective-permute-start.5) | collective-permute-done | bytes 131104 | tf_op jit(solution)/shard_map/ppermute | solution.py:428
  34.2 3.5 %collective-permute-start.6 = (f32[32,768]{1,0:T(8,128)S(1)}, f32[32,768]{1,0:T(8,128)S(1)}, u32[]{:S(2)}, u32[]{:S(2)}) collective-permute-start(f32[32,768]{1,0:T(8,128)S(1)} %shard_map.85.own), channel_id=1, source_target_pairs={{0,24},{1,25},{2,26},{3,27},{4,28},{5,29},{6,30},{7,31},{8,16},{9,... | collective-permute-start | bytes 294920 | tf_op jit(solution)/shard_map/ppermute | solution.py:428
  37.7 3.6 %collective-permute-done.6.other.four = f32[32,768]{1,0:T(8,128)S(1)} collective-permute-done((f32[32,768]{1,0:T(8,128)S(1)}, f32[32,768]{1,0:T(8,128)S(1)}, u32[]{:S(2)}, u32[]{:S(2)}) %collective-permute-start.6) | collective-permute-done | bytes 98336 | tf_op jit(solution)/shard_map/ppermute | solution.py:428
  41.3 2.6 %collective-permute-start.11 = (f32[32,128]{1,0:T(8,128)S(1)}, f32[32,128]{1,0:T(8,128)S(1)}, u32[]{:S(2)}, u32[]{:S(2)}) collective-permute-start(f32[32,128]{1,0:T(8,128)S(1)} %get-tuple-element.49), channel_id=1, source_target_pairs={{0,192},{32,224},{64,128},{96,160},{128,64},{160,96},{192,0},{224,... | collective-permute-start | bytes 49160 | tf_op jit(solution)/shard_map/ppermute | solution.py:428
  48.5 2.8 %collective-permute-start.12 = (f32[32,1280]{1,0:T(8,128)S(1)}, f32[32,1280]{1,0:T(8,128)S(1)}, u32[]{:S(2)}, u32[]{:S(2)}) collective-permute-start(f32[32,1280]{1,0:T(8,128)S(1)} %shard_map.91.b0), channel_id=1, source_target_pairs={{0,1},{1,0},{2,3},{3,2},{4,5},{5,4},{6,7},{7,6},{8,9},{9,8},{10,11... | collective-permute-start | bytes 491528 | tf_op jit(solution)/shard_map/ppermute | solution.py:428
  51.3 3.9 %collective-permute-done.14.b3 = f32[32,1280]{1,0:T(8,128)S(1)} collective-permute-done((f32[32,1280]{1,0:T(8,128)S(1)}, f32[32,1280]{1,0:T(8,128)S(1)}, u32[]{:S(2)}, u32[]{:S(2)}) %collective-permute-start.14) | collective-permute-done | bytes 163872 | tf_op jit(solution)/shard_map/ppermute | solution.py:428
  55.8 5.9 %collective-permute-start.15 = (f32[128,256]{1,0:T(8,128)S(1)}, f32[128,256]{1,0:T(8,128)S(1)}, u32[]{:S(2)}, u32[]{:S(2)}) collective-permute-start(f32[128,256]{1,0:T(8,128)S(1)} %shard_map.92.own_ref), channel_id=1, source_target_pairs={{0,32},{32,0},{64,96},{96,64},{128,160},{160,128},{192,224},{224,1... | collective-permute-start | bytes 393224 | tf_op jit(solution)/shard_map/ppermute | solution.py:428
  71.3 2.4 %collective-permute-done.18.r1 = f32[16,3712]{1,0:T(8,128)S(1)} collective-permute-done((f32[16,3712]{1,0:T(8,128)S(1)}, f32[16,3712]{1,0:T(8,128)S(1)}, u32[]{:S(2)}, u32[]{:S(2)}) %collective-permute-start.18) | collective-permute-done | bytes 237600 | tf_op jit(solution)/shard_map/ppermute | solution.py:428
  73.6 5.5 %collective-permute-done.19.r2 = f32[16,3712]{1,0:T(8,128)S(1)} collective-permute-done((f32[16,3712]{1,0:T(8,128)S(1)}, f32[16,3712]{1,0:T(8,128)S(1)}, u32[]{:S(2)}, u32[]{:S(2)}) %collective-permute-start.19) | collective-permute-done | bytes 237600 | tf_op jit(solution)/shard_map/ppermute | solution.py:428
  81.2 2.3 %collective-permute-start.21 = (f32[16,2688]{1,0:T(8,128)S(1)}, f32[16,2688]{1,0:T(8,128)S(1)}, u32[]{:S(2)}, u32[]{:S(2)}) collective-permute-start(f32[16,2688]{1,0:T(8,128)S(1)} %shard_map.98.own), channel_id=1, source_target_pairs={{0,4},{1,5},{2,6},{3,7},{4,0},{5,1},{6,2},{7,3},{8,12},{9,13},{10,... | collective-permute-start | bytes 516104 | tf_op jit(solution)/shard_map/ppermute | solution.py:428
  83.5 2.8 %collective-permute-done.21.other.two = f32[16,2688]{1,0:T(8,128)S(1)} collective-permute-done((f32[16,2688]{1,0:T(8,128)S(1)}, f32[16,2688]{1,0:T(8,128)S(1)}, u32[]{:S(2)}, u32[]{:S(2)}) %collective-permute-start.21) | collective-permute-done | bytes 172064 | tf_op jit(solution)/shard_map/ppermute | solution.py:428
  86.4 2.7 %collective-permute-start.22 = (f32[16,2176]{1,0:T(8,128)S(1)}, f32[16,2176]{1,0:T(8,128)S(1)}, u32[]{:S(2)}, u32[]{:S(2)}) collective-permute-start(f32[16,2176]{1,0:T(8,128)S(1)} %shard_map.99.own.gate_ref), channel_id=1, source_target_pairs={{0,8},{1,9},{2,10},{3,11},{4,12},{5,13},{6,14},{7,15},{8,0},{9,1},... | collective-permute-start | bytes 417800 | tf_op jit(solution)/shard_map/ppermute | solution.py:428
  89.4 3.2 %collective-permute-start.25 = (f32[16,1536]{1,0:T(8,128)S(1)}, f32[16,1536]{1,0:T(8,128)S(1)}, u32[]{:S(2)}, u32[]{:S(2)}) collective-permute-start(f32[16,1536]{1,0:T(8,128)S(1)} %get-tuple-element.61), channel_id=1, source_target_pairs={{0,2},{1,3},{2,0},{3,1},{4,6},{5,7},{6,4},{7,5},{8,10},{9,11},{10,... | collective-permute-start | bytes 294920 | tf_op jit(solution)/shard_map/ppermute | solution.py:428
  93.3 2.8 %collective-permute-start.23 = (f32[16,1664]{1,0:T(8,128)S(1)}, f32[16,1664]{1,0:T(8,128)S(1)}, u32[]{:S(2)}, u32[]{:S(2)}) collective-permute-start(f32[16,1664]{1,0:T(8,128)S(1)} %shard_map.100.own), channel_id=1, source_target_pairs={{0,24},{1,25},{2,26},{3,27},{4,28},{5,29},{6,30},{7,31},{8,16},{9,... | collective-permute-start | bytes 319496 | tf_op jit(solution)/shard_map/ppermute | solution.py:428
  97.3 4.8 %collective-permute-start.33 = (f32[64,768]{1,0:T(8,128)S(1)}, f32[64,768]{1,0:T(8,128)S(1)}, u32[]{:S(2)}, u32[]{:S(2)}) collective-permute-start(f32[64,768]{1,0:T(8,128)S(1)} %get-tuple-element.67), channel_id=1, source_target_pairs={{0,32},{32,0},{64,96},{96,64},{128,160},{160,128},{192,224},{224,1... | collective-permute-start | bytes 589832 | tf_op jit(solution)/shard_map/ppermute | solution.py:428
  108.8 2.4 %collective-permute-start.30 = (f32[16,2176]{1,0:T(8,128)S(1)}, f32[16,2176]{1,0:T(8,128)S(1)}, u32[]{:S(2)}, u32[]{:S(2)}) collective-permute-start(f32[16,2176]{1,0:T(8,128)S(1)} %shard_map.103.b0), channel_id=1, source_target_pairs={{0,1},{1,0},{2,3},{3,2},{4,5},{5,4},{6,7},{7,6},{8,9},{9,8},{10,11... | collective-permute-start | bytes 417800 | tf_op jit(solution)/shard_map/ppermute | solution.py:428
  111.8 2.7 %collective-permute-done.32.b3 = f32[16,2176]{1,0:T(8,128)S(1)} collective-permute-done((f32[16,2176]{1,0:T(8,128)S(1)}, f32[16,2176]{1,0:T(8,128)S(1)}, u32[]{:S(2)}, u32[]{:S(2)}) %collective-permute-start.32) | collective-permute-done | bytes 139296 | tf_op jit(solution)/shard_map/ppermute | solution.py:428
  115.2 5.2 %collective-permute-start.34 = (f32[64,1408]{1,0:T(8,128)S(1)}, f32[64,1408]{1,0:T(8,128)S(1)}, u32[]{:S(2)}, u32[]{:S(2)}) collective-permute-start(f32[64,1408]{1,0:T(8,128)S(1)} %get-tuple-element.69), channel_id=1, source_target_pairs={{0,32},{32,0},{64,96},{96,64},{128,160},{160,128},{192,224},{224,1... | collective-permute-start | bytes 1081352 | tf_op jit(solution)/shard_map/ppermute | solution.py:428
  (93 shorter events, 41.9 us)
Async XLA Ops:
  9.3 9.3 %collective-permute-start.1 = (f32[32,1280]{1,0:T(8,128)S(1)}, f32[32,1280]{1,0:T(8,128)S(1)}, u32[]{:S(2)}, u32[]{:S(2)}) collective-permute-start(f32[32,1280]{1,0:T(8,128)S(1)} %get-tuple-element.40), channel_id=1, source_target_pairs={{0,1},{1,0},{2,3},{3,2},{4,5},{5,4},{6,7},{7,6},{8,9},{9,8},{10,11... | collective-permute-start | bytes 491528 | tf_op jit(solution)/shard_map/ppermute | solution.py:428
  9.4 9.7 %collective-permute-start.2 = (f32[32,1280]{1,0:T(8,128)S(1)}, f32[32,1280]{1,0:T(8,128)S(1)}, u32[]{:S(2)}, u32[]{:S(2)}) collective-permute-start(f32[32,1280]{1,0:T(8,128)S(1)} %get-tuple-element.41), channel_id=1, source_target_pairs={{0,2},{1,3},{2,0},{3,1},{4,6},{5,7},{6,4},{7,5},{8,10},{9,11},{10,... | collective-permute-start | bytes 491528 | tf_op jit(solution)/shard_map/ppermute | solution.py:428
  11.6 10.2 %collective-permute-start.3 = (f32[32,1280]{1,0:T(8,128)S(1)}, f32[32,1280]{1,0:T(8,128)S(1)}, u32[]{:S(2)}, u32[]{:S(2)}) collective-permute-start(f32[32,1280]{1,0:T(8,128)S(1)} %get-tuple-element.42), channel_id=1, source_target_pairs={{0,3},{1,2},{2,1},{3,0},{4,7},{5,6},{6,5},{7,4},{8,11},{9,10},{10,... | collective-permute-start | bytes 491528 | tf_op jit(solution)/shard_map/ppermute | solution.py:428
  23.9 6.4 %collective-permute-start.7 = (f32[128,512]{1,0:T(8,128)S(1)}, f32[128,512]{1,0:T(8,128)S(1)}, u32[]{:S(2)}, u32[]{:S(2)}) collective-permute-start(f32[128,512]{1,0:T(8,128)S(1)} %shard_map.86.own), channel_id=1, source_target_pairs={{0,1},{1,0},{2,3},{3,2},{4,5},{5,4},{6,7},{7,6},{8,9},{9,8},{10,11... | collective-permute-start | bytes 786440 | tf_op jit(solution)/shard_map/ppermute | solution.py:428
  26.8 7.4 %collective-permute-start.5 = (f32[32,1024]{1,0:T(8,128)S(1)}, f32[32,1024]{1,0:T(8,128)S(1)}, u32[]{:S(2)}, u32[]{:S(2)}) collective-permute-start(f32[32,1024]{1,0:T(8,128)S(1)} %shard_map.84.own), channel_id=1, source_target_pairs={{0,8},{1,9},{2,10},{3,11},{4,12},{5,13},{6,14},{7,15},{8,0},{9,1},... | collective-permute-start | bytes 393224 | tf_op jit(solution)/shard_map/ppermute | solution.py:428
  30.3 11.0 %collective-permute-start.8 = (f32[128,256]{1,0:T(8,128)S(1)}, f32[128,256]{1,0:T(8,128)S(1)}, u32[]{:S(2)}, u32[]{:S(2)}) collective-permute-start(f32[128,256]{1,0:T(8,128)S(1)} %shard_map.87), channel_id=1, source_target_pairs={{0,3},{1,2},{2,1},{3,0},{4,7},{5,6},{6,5},{7,4},{8,11},{9,10},{10,... | collective-permute-start | bytes 393224 | tf_op jit(solution)/shard_map/ppermute | solution.py:428
  34.2 7.1 %collective-permute-start.6 = (f32[32,768]{1,0:T(8,128)S(1)}, f32[32,768]{1,0:T(8,128)S(1)}, u32[]{:S(2)}, u32[]{:S(2)}) collective-permute-start(f32[32,768]{1,0:T(8,128)S(1)} %shard_map.85.own), channel_id=1, source_target_pairs={{0,24},{1,25},{2,26},{3,27},{4,28},{5,29},{6,30},{7,31},{8,16},{9,... | collective-permute-start | bytes 294920 | tf_op jit(solution)/shard_map/ppermute | solution.py:428
  41.3 5.7 %collective-permute-start.11 = (f32[32,128]{1,0:T(8,128)S(1)}, f32[32,128]{1,0:T(8,128)S(1)}, u32[]{:S(2)}, u32[]{:S(2)}) collective-permute-start(f32[32,128]{1,0:T(8,128)S(1)} %get-tuple-element.49), channel_id=1, source_target_pairs={{0,192},{32,224},{64,128},{96,160},{128,64},{160,96},{192,0},{224,... | collective-permute-start | bytes 49160 | tf_op jit(solution)/shard_map/ppermute | solution.py:428
  48.0 7.2 %collective-permute-start.14 = (f32[32,1280]{1,0:T(8,128)S(1)}, f32[32,1280]{1,0:T(8,128)S(1)}, u32[]{:S(2)}, u32[]{:S(2)}) collective-permute-start(f32[32,1280]{1,0:T(8,128)S(1)} %shard_map.91.b0), channel_id=1, source_target_pairs={{0,3},{1,2},{2,1},{3,0},{4,7},{5,6},{6,5},{7,4},{8,11},{9,10},{10,... | collective-permute-start | bytes 491528 | tf_op jit(solution)/shard_map/ppermute | solution.py:428
  48.5 6.7 %collective-permute-start.13 = (f32[32,1280]{1,0:T(8,128)S(1)}, f32[32,1280]{1,0:T(8,128)S(1)}, u32[]{:S(2)}, u32[]{:S(2)}) collective-permute-start(f32[32,1280]{1,0:T(8,128)S(1)} %shard_map.91.b0), channel_id=1, source_target_pairs={{0,2},{1,3},{2,0},{3,1},{4,6},{5,7},{6,4},{7,5},{8,10},{9,11},{10,... | collective-permute-start | bytes 491528 | tf_op jit(solution)/shard_map/ppermute | solution.py:428
  48.5 7.3 %collective-permute-start.12 = (f32[32,1280]{1,0:T(8,128)S(1)}, f32[32,1280]{1,0:T(8,128)S(1)}, u32[]{:S(2)}, u32[]{:S(2)}) collective-permute-start(f32[32,1280]{1,0:T(8,128)S(1)} %shard_map.91.b0), channel_id=1, source_target_pairs={{0,1},{1,0},{2,3},{3,2},{4,5},{5,4},{6,7},{7,6},{8,9},{9,8},{10,11... | collective-permute-start | bytes 491528 | tf_op jit(solution)/shard_map/ppermute | solution.py:428
  55.8 6.8 %collective-permute-start.15 = (f32[128,256]{1,0:T(8,128)S(1)}, f32[128,256]{1,0:T(8,128)S(1)}, u32[]{:S(2)}, u32[]{:S(2)}) collective-permute-start(f32[128,256]{1,0:T(8,128)S(1)} %shard_map.92.own_ref), channel_id=1, source_target_pairs={{0,32},{32,0},{64,96},{96,64},{128,160},{160,128},{192,224},{224,1... | collective-permute-start | bytes 393224 | tf_op jit(solution)/shard_map/ppermute | solution.py:428
  66.3 7.3 %collective-permute-start.18 = (f32[16,3712]{1,0:T(8,128)S(1)}, f32[16,3712]{1,0:T(8,128)S(1)}, u32[]{:S(2)}, u32[]{:S(2)}) collective-permute-start(f32[16,3712]{1,0:T(8,128)S(1)} %get-tuple-element.57), channel_id=1, source_target_pairs={{0,1},{1,0},{2,3},{3,2},{4,5},{5,4},{6,7},{7,6},{8,9},{9,8},{10,11... | collective-permute-start | bytes 712712 | tf_op jit(solution)/shard_map/ppermute | solution.py:428
  66.4 12.7 %collective-permute-start.19 = (f32[16,3712]{1,0:T(8,128)S(1)}, f32[16,3712]{1,0:T(8,128)S(1)}, u32[]{:S(2)}, u32[]{:S(2)}) collective-permute-start(f32[16,3712]{1,0:T(8,128)S(1)} %get-tuple-element.58), channel_id=1, source_target_pairs={{0,2},{1,3},{2,0},{3,1},{4,6},{5,7},{6,4},{7,5},{8,10},{9,11},{10,... | collective-permute-start | bytes 712712 | tf_op jit(solution)/shard_map/ppermute | solution.py:428
  68.2 12.9 %collective-permute-start.20 = (f32[16,3712]{1,0:T(8,128)S(1)}, f32[16,3712]{1,0:T(8,128)S(1)}, u32[]{:S(2)}, u32[]{:S(2)}) collective-permute-start(f32[16,3712]{1,0:T(8,128)S(1)} %get-tuple-element.59), channel_id=1, source_target_pairs={{0,3},{1,2},{2,1},{3,0},{4,7},{5,6},{6,5},{7,4},{8,11},{9,10},{10,... | collective-permute-start | bytes 712712 | tf_op jit(solution)/shard_map/ppermute | solution.py:428
  86.4 6.9 %collective-permute-start.22 = (f32[16,2176]{1,0:T(8,128)S(1)}, f32[16,2176]{1,0:T(8,128)S(1)}, u32[]{:S(2)}, u32[]{:S(2)}) collective-permute-start(f32[16,2176]{1,0:T(8,128)S(1)} %shard_map.99.own.gate_ref), channel_id=1, source_target_pairs={{0,8},{1,9},{2,10},{3,11},{4,12},{5,13},{6,14},{7,15},{8,0},{9,1},... | collective-permute-start | bytes 417800 | tf_op jit(solution)/shard_map/ppermute | solution.py:428
  89.1 7.1 %collective-permute-start.24 = (f32[16,1536]{1,0:T(8,128)S(1)}, f32[16,1536]{1,0:T(8,128)S(1)}, u32[]{:S(2)}, u32[]{:S(2)}) collective-permute-start(f32[16,1536]{1,0:T(8,128)S(1)} %get-tuple-element.60), channel_id=1, source_target_pairs={{0,1},{1,0},{2,3},{3,2},{4,5},{5,4},{6,7},{7,6},{8,9},{9,8},{10,11... | collective-permute-start | bytes 294920 | tf_op jit(solution)/shard_map/ppermute | solution.py:428
  89.4 6.8 %collective-permute-start.25 = (f32[16,1536]{1,0:T(8,128)S(1)}, f32[16,1536]{1,0:T(8,128)S(1)}, u32[]{:S(2)}, u32[]{:S(2)}) collective-permute-start(f32[16,1536]{1,0:T(8,128)S(1)} %get-tuple-element.61), channel_id=1, source_target_pairs={{0,2},{1,3},{2,0},{3,1},{4,6},{5,7},{6,4},{7,5},{8,10},{9,11},{10,... | collective-permute-start | bytes 294920 | tf_op jit(solution)/shard_map/ppermute | solution.py:428
  93.3 8.8 %collective-permute-start.23 = (f32[16,1664]{1,0:T(8,128)S(1)}, f32[16,1664]{1,0:T(8,128)S(1)}, u32[]{:S(2)}, u32[]{:S(2)}) collective-permute-start(f32[16,1664]{1,0:T(8,128)S(1)} %shard_map.100.own), channel_id=1, source_target_pairs={{0,24},{1,25},{2,26},{3,27},{4,28},{5,29},{6,30},{7,31},{8,16},{9,... | collective-permute-start | bytes 319496 | tf_op jit(solution)/shard_map/ppermute | solution.py:428
  97.3 13.9 %collective-permute-start.33 = (f32[64,768]{1,0:T(8,128)S(1)}, f32[64,768]{1,0:T(8,128)S(1)}, u32[]{:S(2)}, u32[]{:S(2)}) collective-permute-start(f32[64,768]{1,0:T(8,128)S(1)} %get-tuple-element.67), channel_id=1, source_target_pairs={{0,32},{32,0},{64,96},{96,64},{128,160},{160,128},{192,224},{224,1... | collective-permute-start | bytes 589832 | tf_op jit(solution)/shard_map/ppermute | solution.py:428
  107.8 6.7 %collective-permute-start.32 = (f32[16,2176]{1,0:T(8,128)S(1)}, f32[16,2176]{1,0:T(8,128)S(1)}, u32[]{:S(2)}, u32[]{:S(2)}) collective-permute-start(f32[16,2176]{1,0:T(8,128)S(1)} %shard_map.103.b0), channel_id=1, source_target_pairs={{0,3},{1,2},{2,1},{3,0},{4,7},{5,6},{6,5},{7,4},{8,11},{9,10},{10,... | collective-permute-start | bytes 417800 | tf_op jit(solution)/shard_map/ppermute | solution.py:428
  108.6 6.0 %collective-permute-start.31 = (f32[16,2176]{1,0:T(8,128)S(1)}, f32[16,2176]{1,0:T(8,128)S(1)}, u32[]{:S(2)}, u32[]{:S(2)}) collective-permute-start(f32[16,2176]{1,0:T(8,128)S(1)} %shard_map.103.b0), channel_id=1, source_target_pairs={{0,2},{1,3},{2,0},{3,1},{4,6},{5,7},{6,4},{7,5},{8,10},{9,11},{10,... | collective-permute-start | bytes 417800 | tf_op jit(solution)/shard_map/ppermute | solution.py:428
  108.8 6.3 %collective-permute-start.30 = (f32[16,2176]{1,0:T(8,128)S(1)}, f32[16,2176]{1,0:T(8,128)S(1)}, u32[]{:S(2)}, u32[]{:S(2)}) collective-permute-start(f32[16,2176]{1,0:T(8,128)S(1)} %shard_map.103.b0), channel_id=1, source_target_pairs={{0,1},{1,0},{2,3},{3,2},{4,5},{5,4},{6,7},{7,6},{8,9},{9,8},{10,11... | collective-permute-start | bytes 417800 | tf_op jit(solution)/shard_map/ppermute | solution.py:428
  115.2 6.5 %collective-permute-start.34 = (f32[64,1408]{1,0:T(8,128)S(1)}, f32[64,1408]{1,0:T(8,128)S(1)}, u32[]{:S(2)}, u32[]{:S(2)}) collective-permute-start(f32[64,1408]{1,0:T(8,128)S(1)} %get-tuple-element.69), channel_id=1, source_target_pairs={{0,32},{32,0},{64,96},{96,64},{128,160},{160,128},{192,224},{224,1... | collective-permute-start | bytes 1081352 | tf_op jit(solution)/shard_map/ppermute | solution.py:428
  (17 other events, 91.1 us)
where the time goes:
time: 124 us
  starting transfers between devices  61.6 us (50%)
  waiting for transfers between devices  42.7 us (34%)
  Pallas kernels  18.2 us (15%)
    ppermute x35, starting transfers between devices, swap(): lax.ppermute(x, axis, [(i, i ^ mask) for i in range(lax.axis_size(axis))])  61.6 us
    ppermute x35, waiting for transfers between devices, swap(): lax.ppermute(x, axis, [(i, i ^ mask) for i in range(lax.axis_size(axis))])  42.7 us
    pallas_call x31, Pallas kernels, call(): pl.pallas_call(kernel, out_shape=out_shape, in_specs=[SMEM] * smem + [VME...  18.2 us
  transfers between devices with their start and end apart: 35, of which 23 were waited for; matrix products, arithmetic and copies ran while one was open for 0% of the time, Pallas kernels for 9%

commit v1 on v0

--- a/solution.py
+++ b/solution.py
@@ -18,7 +18,7 @@
 PART = PROBES // 4
 ROWS = PART // 2
 LANES = 128
-CHUNKS = 4
+CHUNKS = 2
 START_LIMIT = 52
 F32 = jnp.float32
 BF16 = jnp.bfloat16

time: 124 us -> 124 us (level)
  no operation moved by 1% of the time
where the time goes in v1:
time: 124 us
  starting transfers between devices  61.6 us (50%)
  waiting for transfers between devices  42.6 us (34%)
  Pallas kernels  18.5 us (15%)
    ppermute x35, starting transfers between devices, swap(): lax.ppermute(x, axis, [(i, i ^ mask) for i in range(lax.axis_size(axis))])  61.6 us
    ppermute x35, waiting for transfers between devices, swap(): lax.ppermute(x, axis, [(i, i ^ mask) for i in range(lax.axis_size(axis))])  42.6 us
    pallas_call x31, Pallas kernels, call(): pl.pallas_call(kernel, out_shape=out_shape, in_specs=[SMEM] * smem + [VME...  18.5 us
  transfers between devices with their start and end apart: 35, of which 23 were waited for; matrix products, arithmetic and copies ran while one was open for 0% of the time, Pallas kernels for 9%

profile of v1, /device:TPU:1, one launch (start us, length us, event | category | flops | bytes accessed | tf_op | source)
XLA Modules:
  0.0 123.9 jit_solution(16727213958475246042)
XLA Ops:
  0.7 4.4 %shard_map.77 = (bf16[8,1024,256]{2,1,0:T(8,128)(2,1)}, f32[128,512]{1,0:T(8,128)S(1)}, f32[128,256]{1,0:T(8,128)S(1)}, f32[128,768]{1,0:T(8,128)S(1)}) custom-call(s32[1]{0:T(128)} %bitcast.core_ref, f32[128,1024]{1,0:T(8,128)} %v_ref.9, bf16[8192,256]{1,0:T(8,128)(2,1)} %bitcast.5), custom_call_target="tpu_custom_call" | custom-call | flops 2147483648 | bytes 1048576 | tf_op jit(solution)/shard_map/pallas_call | solution.py:37
  5.1 3.3 %collective-permute-start = (f32[128,512]{1,0:T(8,128)S(1)}, f32[128,512]{1,0:T(8,128)S(1)}, u32[]{:S(2)}, u32[]{:S(2)}) collective-permute-start(f32[128,512]{1,0:T(8,128)S(1)} %get-tuple-element.38), channel_id=1, source_target_pairs={{0,32},{32,0},{64,96},{96,64},{128,160},{160,128},{192,224},{224,1... | collective-permute-start | bytes 786440 | tf_op jit(solution)/shard_map/ppermute | solution.py:428
  9.7 2.2 %collective-permute-start.2 = (f32[32,1280]{1,0:T(8,128)S(1)}, f32[32,1280]{1,0:T(8,128)S(1)}, u32[]{:S(2)}, u32[]{:S(2)}) collective-permute-start(f32[32,1280]{1,0:T(8,128)S(1)} %get-tuple-element.41), channel_id=1, source_target_pairs={{0,2},{1,3},{2,0},{3,1},{4,6},{5,7},{6,4},{7,5},{8,10},{9,11},{10,... | collective-permute-start | bytes 491528 | tf_op jit(solution)/shard_map/ppermute | solution.py:428
  19.4 2.7 %collective-permute-done.3.r3 = f32[32,1280]{1,0:T(8,128)S(1)} collective-permute-done((f32[32,1280]{1,0:T(8,128)S(1)}, f32[32,1280]{1,0:T(8,128)S(1)}, u32[]{:S(2)}, u32[]{:S(2)}) %collective-permute-start.3) | collective-permute-done | bytes 163872 | tf_op jit(solution)/shard_map/ppermute | solution.py:428
  24.3 2.8 %collective-permute-done.4.other.two = f32[32,1280]{1,0:T(8,128)S(1)} collective-permute-done((f32[32,1280]{1,0:T(8,128)S(1)}, f32[32,1280]{1,0:T(8,128)S(1)}, u32[]{:S(2)}, u32[]{:S(2)}) %collective-permute-start.4) | collective-permute-done | bytes 163872 | tf_op jit(solution)/shard_map/ppermute | solution.py:428
  27.1 3.1 %collective-permute-start.5 = (f32[32,1024]{1,0:T(8,128)S(1)}, f32[32,1024]{1,0:T(8,128)S(1)}, u32[]{:S(2)}, u32[]{:S(2)}) collective-permute-start(f32[32,1024]{1,0:T(8,128)S(1)} %shard_map.84.own), channel_id=1, source_target_pairs={{0,8},{1,9},{2,10},{3,11},{4,12},{5,13},{6,14},{7,15},{8,0},{9,1},... | collective-permute-start | bytes 393224 | tf_op jit(solution)/shard_map/ppermute | solution.py:428
  30.9 3.6 %collective-permute-done.5.other.three = f32[32,1024]{1,0:T(8,128)S(1)} collective-permute-done((f32[32,1024]{1,0:T(8,128)S(1)}, f32[32,1024]{1,0:T(8,128)S(1)}, u32[]{:S(2)}, u32[]{:S(2)}) %collective-permute-start.5) | collective-permute-done | bytes 131104 | tf_op jit(solution)/shard_map/ppermute | solution.py:428
  34.5 3.5 %collective-permute-start.6 = (f32[32,768]{1,0:T(8,128)S(1)}, f32[32,768]{1,0:T(8,128)S(1)}, u32[]{:S(2)}, u32[]{:S(2)}) collective-permute-start(f32[32,768]{1,0:T(8,128)S(1)} %shard_map.85.own), channel_id=1, source_target_pairs={{0,24},{1,25},{2,26},{3,27},{4,28},{5,29},{6,30},{7,31},{8,16},{9,... | collective-permute-start | bytes 294920 | tf_op jit(solution)/shard_map/ppermute | solution.py:428
  38.0 3.6 %collective-permute-done.6.other.four = f32[32,768]{1,0:T(8,128)S(1)} collective-permute-done((f32[32,768]{1,0:T(8,128)S(1)}, f32[32,768]{1,0:T(8,128)S(1)}, u32[]{:S(2)}, u32[]{:S(2)}) %collective-permute-start.6) | collective-permute-done | bytes 98336 | tf_op jit(solution)/shard_map/ppermute | solution.py:428
  41.6 2.6 %collective-permute-start.11 = (f32[32,128]{1,0:T(8,128)S(1)}, f32[32,128]{1,0:T(8,128)S(1)}, u32[]{:S(2)}, u32[]{:S(2)}) collective-permute-start(f32[32,128]{1,0:T(8,128)S(1)} %get-tuple-element.49), channel_id=1, source_target_pairs={{0,192},{32,224},{64,128},{96,160},{128,64},{160,96},{192,0},{224,... | collective-permute-start | bytes 49160 | tf_op jit(solution)/shard_map/ppermute | solution.py:428
  48.8 2.8 %collective-permute-start.12 = (f32[32,1280]{1,0:T(8,128)S(1)}, f32[32,1280]{1,0:T(8,128)S(1)}, u32[]{:S(2)}, u32[]{:S(2)}) collective-permute-start(f32[32,1280]{1,0:T(8,128)S(1)} %shard_map.91.b0), channel_id=1, source_target_pairs={{0,1},{1,0},{2,3},{3,2},{4,5},{5,4},{6,7},{7,6},{8,9},{9,8},{10,11... | collective-permute-start | bytes 491528 | tf_op jit(solution)/shard_map/ppermute | solution.py:428
  51.6 3.9 %collective-permute-done.14.b3 = f32[32,1280]{1,0:T(8,128)S(1)} collective-permute-done((f32[32,1280]{1,0:T(8,128)S(1)}, f32[32,1280]{1,0:T(8,128)S(1)}, u32[]{:S(2)}, u32[]{:S(2)}) %collective-permute-start.14) | collective-permute-done | bytes 163872 | tf_op jit(solution)/shard_map/ppermute | solution.py:428
  56.1 5.9 %collective-permute-start.15 = (f32[128,256]{1,0:T(8,128)S(1)}, f32[128,256]{1,0:T(8,128)S(1)}, u32[]{:S(2)}, u32[]{:S(2)}) collective-permute-start(f32[128,256]{1,0:T(8,128)S(1)} %shard_map.92.own_ref), channel_id=1, source_target_pairs={{0,32},{32,0},{64,96},{96,64},{128,160},{160,128},{192,224},{224,1... | collective-permute-start | bytes 393224 | tf_op jit(solution)/shard_map/ppermute | solution.py:428
  71.6 2.4 %collective-permute-done.18.r1 = f32[16,3712]{1,0:T(8,128)S(1)} collective-permute-done((f32[16,3712]{1,0:T(8,128)S(1)}, f32[16,3712]{1,0:T(8,128)S(1)}, u32[]{:S(2)}, u32[]{:S(2)}) %collective-permute-start.18) | collective-permute-done | bytes 237600 | tf_op jit(solution)/shard_map/ppermute | solution.py:428
  73.9 5.5 %collective-permute-done.19.r2 = f32[16,3712]{1,0:T(8,128)S(1)} collective-permute-done((f32[16,3712]{1,0:T(8,128)S(1)}, f32[16,3712]{1,0:T(8,128)S(1)}, u32[]{:S(2)}, u32[]{:S(2)}) %collective-permute-start.19) | collective-permute-done | bytes 237600 | tf_op jit(solution)/shard_map/ppermute | solution.py:428
  81.5 2.3 %collective-permute-start.21 = (f32[16,2688]{1,0:T(8,128)S(1)}, f32[16,2688]{1,0:T(8,128)S(1)}, u32[]{:S(2)}, u32[]{:S(2)}) collective-permute-start(f32[16,2688]{1,0:T(8,128)S(1)} %shard_map.98.own), channel_id=1, source_target_pairs={{0,4},{1,5},{2,6},{3,7},{4,0},{5,1},{6,2},{7,3},{8,12},{9,13},{10,... | collective-permute-start | bytes 516104 | tf_op jit(solution)/shard_map/ppermute | solution.py:428
  83.8 2.8 %collective-permute-done.21.other.two = f32[16,2688]{1,0:T(8,128)S(1)} collective-permute-done((f32[16,2688]{1,0:T(8,128)S(1)}, f32[16,2688]{1,0:T(8,128)S(1)}, u32[]{:S(2)}, u32[]{:S(2)}) %collective-permute-start.21) | collective-permute-done | bytes 172064 | tf_op jit(solution)/shard_map/ppermute | solution.py:428
  86.7 2.7 %collective-permute-start.22 = (f32[16,2176]{1,0:T(8,128)S(1)}, f32[16,2176]{1,0:T(8,128)S(1)}, u32[]{:S(2)}, u32[]{:S(2)}) collective-permute-start(f32[16,2176]{1,0:T(8,128)S(1)} %shard_map.99.own.gate_ref), channel_id=1, source_target_pairs={{0,8},{1,9},{2,10},{3,11},{4,12},{5,13},{6,14},{7,15},{8,0},{9,1},... | collective-permute-start | bytes 417800 | tf_op jit(solution)/shard_map/ppermute | solution.py:428
  89.7 3.2 %collective-permute-start.25 = (f32[16,1536]{1,0:T(8,128)S(1)}, f32[16,1536]{1,0:T(8,128)S(1)}, u32[]{:S(2)}, u32[]{:S(2)}) collective-permute-start(f32[16,1536]{1,0:T(8,128)S(1)} %get-tuple-element.61), channel_id=1, source_target_pairs={{0,2},{1,3},{2,0},{3,1},{4,6},{5,7},{6,4},{7,5},{8,10},{9,11},{10,... | collective-permute-start | bytes 294920 | tf_op jit(solution)/shard_map/ppermute | solution.py:428
  93.7 2.8 %collective-permute-start.23 = (f32[16,1664]{1,0:T(8,128)S(1)}, f32[16,1664]{1,0:T(8,128)S(1)}, u32[]{:S(2)}, u32[]{:S(2)}) collective-permute-start(f32[16,1664]{1,0:T(8,128)S(1)} %shard_map.100.own), channel_id=1, source_target_pairs={{0,24},{1,25},{2,26},{3,27},{4,28},{5,29},{6,30},{7,31},{8,16},{9,... | collective-permute-start | bytes 319496 | tf_op jit(solution)/shard_map/ppermute | solution.py:428
  97.6 4.8 %collective-permute-start.33 = (f32[64,768]{1,0:T(8,128)S(1)}, f32[64,768]{1,0:T(8,128)S(1)}, u32[]{:S(2)}, u32[]{:S(2)}) collective-permute-start(f32[64,768]{1,0:T(8,128)S(1)} %get-tuple-element.67), channel_id=1, source_target_pairs={{0,32},{32,0},{64,96},{96,64},{128,160},{160,128},{192,224},{224,1... | collective-permute-start | bytes 589832 | tf_op jit(solution)/shard_map/ppermute | solution.py:428
  109.1 2.4 %collective-permute-start.30 = (f32[16,2176]{1,0:T(8,128)S(1)}, f32[16,2176]{1,0:T(8,128)S(1)}, u32[]{:S(2)}, u32[]{:S(2)}) collective-permute-start(f32[16,2176]{1,0:T(8,128)S(1)} %shard_map.103.b0), channel_id=1, source_target_pairs={{0,1},{1,0},{2,3},{3,2},{4,5},{5,4},{6,7},{7,6},{8,9},{9,8},{10,11... | collective-permute-start | bytes 417800 | tf_op jit(solution)/shard_map/ppermute | solution.py:428
  112.2 2.7 %collective-permute-done.32.b3 = f32[16,2176]{1,0:T(8,128)S(1)} collective-permute-done((f32[16,2176]{1,0:T(8,128)S(1)}, f32[16,2176]{1,0:T(8,128)S(1)}, u32[]{:S(2)}, u32[]{:S(2)}) %collective-permute-start.32) | collective-permute-done | bytes 139296 | tf_op jit(solution)/shard_map/ppermute | solution.py:428
  115.5 5.2 %collective-permute-start.34 = (f32[64,1408]{1,0:T(8,128)S(1)}, f32[64,1408]{1,0:T(8,128)S(1)}, u32[]{:S(2)}, u32[]{:S(2)}) collective-permute-start(f32[64,1408]{1,0:T(8,128)S(1)} %get-tuple-element.69), channel_id=1, source_target_pairs={{0,32},{32,0},{64,96},{96,64},{128,160},{160,128},{192,224},{224,1... | collective-permute-start | bytes 1081352 | tf_op jit(solution)/shard_map/ppermute | solution.py:428
  (93 shorter events, 41.9 us)
Async XLA Ops:
  9.6 9.3 %collective-permute-start.1 = (f32[32,1280]{1,0:T(8,128)S(1)}, f32[32,1280]{1,0:T(8,128)S(1)}, u32[]{:S(2)}, u32[]{:S(2)}) collective-permute-start(f32[32,1280]{1,0:T(8,128)S(1)} %get-tuple-element.40), channel_id=1, source_target_pairs={{0,1},{1,0},{2,3},{3,2},{4,5},{5,4},{6,7},{7,6},{8,9},{9,8},{10,11... | collective-permute-start | bytes 491528 | tf_op jit(solution)/shard_map/ppermute | solution.py:428
  9.7 9.7 %collective-permute-start.2 = (f32[32,1280]{1,0:T(8,128)S(1)}, f32[32,1280]{1,0:T(8,128)S(1)}, u32[]{:S(2)}, u32[]{:S(2)}) collective-permute-start(f32[32,1280]{1,0:T(8,128)S(1)} %get-tuple-element.41), channel_id=1, source_target_pairs={{0,2},{1,3},{2,0},{3,1},{4,6},{5,7},{6,4},{7,5},{8,10},{9,11},{10,... | collective-permute-start | bytes 491528 | tf_op jit(solution)/shard_map/ppermute | solution.py:428
  11.9 10.2 %collective-permute-start.3 = (f32[32,1280]{1,0:T(8,128)S(1)}, f32[32,1280]{1,0:T(8,128)S(1)}, u32[]{:S(2)}, u32[]{:S(2)}) collective-permute-start(f32[32,1280]{1,0:T(8,128)S(1)} %get-tuple-element.42), channel_id=1, source_target_pairs={{0,3},{1,2},{2,1},{3,0},{4,7},{5,6},{6,5},{7,4},{8,11},{9,10},{10,... | collective-permute-start | bytes 491528 | tf_op jit(solution)/shard_map/ppermute | solution.py:428
  24.2 6.4 %collective-permute-start.7 = (f32[128,512]{1,0:T(8,128)S(1)}, f32[128,512]{1,0:T(8,128)S(1)}, u32[]{:S(2)}, u32[]{:S(2)}) collective-permute-start(f32[128,512]{1,0:T(8,128)S(1)} %shard_map.86.own), channel_id=1, source_target_pairs={{0,1},{1,0},{2,3},{3,2},{4,5},{5,4},{6,7},{7,6},{8,9},{9,8},{10,11... | collective-permute-start | bytes 786440 | tf_op jit(solution)/shard_map/ppermute | solution.py:428
  27.1 7.4 %collective-permute-start.5 = (f32[32,1024]{1,0:T(8,128)S(1)}, f32[32,1024]{1,0:T(8,128)S(1)}, u32[]{:S(2)}, u32[]{:S(2)}) collective-permute-start(f32[32,1024]{1,0:T(8,128)S(1)} %shard_map.84.own), channel_id=1, source_target_pairs={{0,8},{1,9},{2,10},{3,11},{4,12},{5,13},{6,14},{7,15},{8,0},{9,1},... | collective-permute-start | bytes 393224 | tf_op jit(solution)/shard_map/ppermute | solution.py:428
  30.6 10.9 %collective-permute-start.8 = (f32[128,256]{1,0:T(8,128)S(1)}, f32[128,256]{1,0:T(8,128)S(1)}, u32[]{:S(2)}, u32[]{:S(2)}) collective-permute-start(f32[128,256]{1,0:T(8,128)S(1)} %shard_map.87), channel_id=1, source_target_pairs={{0,3},{1,2},{2,1},{3,0},{4,7},{5,6},{6,5},{7,4},{8,11},{9,10},{10,... | collective-permute-start | bytes 393224 | tf_op jit(solution)/shard_map/ppermute | solution.py:428
  34.5 7.1 %collective-permute-start.6 = (f32[32,768]{1,0:T(8,128)S(1)}, f32[32,768]{1,0:T(8,128)S(1)}, u32[]{:S(2)}, u32[]{:S(2)}) collective-permute-start(f32[32,768]{1,0:T(8,128)S(1)} %shard_map.85.own), channel_id=1, source_target_pairs={{0,24},{1,25},{2,26},{3,27},{4,28},{5,29},{6,30},{7,31},{8,16},{9,... | collective-permute-start | bytes 294920 | tf_op jit(solution)/shard_map/ppermute | solution.py:428
  41.6 5.7 %collective-permute-start.11 = (f32[32,128]{1,0:T(8,128)S(1)}, f32[32,128]{1,0:T(8,128)S(1)}, u32[]{:S(2)}, u32[]{:S(2)}) collective-permute-start(f32[32,128]{1,0:T(8,128)S(1)} %get-tuple-element.49), channel_id=1, source_target_pairs={{0,192},{32,224},{64,128},{96,160},{128,64},{160,96},{192,0},{224,... | collective-permute-start | bytes 49160 | tf_op jit(solution)/shard_map/ppermute | solution.py:428
  48.3 7.2 %collective-permute-start.14 = (f32[32,1280]{1,0:T(8,128)S(1)}, f32[32,1280]{1,0:T(8,128)S(1)}, u32[]{:S(2)}, u32[]{:S(2)}) collective-permute-start(f32[32,1280]{1,0:T(8,128)S(1)} %shard_map.91.b0), channel_id=1, source_target_pairs={{0,3},{1,2},{2,1},{3,0},{4,7},{5,6},{6,5},{7,4},{8,11},{9,10},{10,... | collective-permute-start | bytes 491528 | tf_op jit(solution)/shard_map/ppermute | solution.py:428
  48.8 6.7 %collective-permute-start.13 = (f32[32,1280]{1,0:T(8,128)S(1)}, f32[32,1280]{1,0:T(8,128)S(1)}, u32[]{:S(2)}, u32[]{:S(2)}) collective-permute-start(f32[32,1280]{1,0:T(8,128)S(1)} %shard_map.91.b0), channel_id=1, source_target_pairs={{0,2},{1,3},{2,0},{3,1},{4,6},{5,7},{6,4},{7,5},{8,10},{9,11},{10,... | collective-permute-start | bytes 491528 | tf_op jit(solution)/shard_map/ppermute | solution.py:428
  48.8 7.3 %collective-permute-start.12 = (f32[32,1280]{1,0:T(8,128)S(1)}, f32[32,1280]{1,0:T(8,128)S(1)}, u32[]{:S(2)}, u32[]{:S(2)}) collective-permute-start(f32[32,1280]{1,0:T(8,128)S(1)} %shard_map.91.b0), channel_id=1, source_target_pairs={{0,1},{1,0},{2,3},{3,2},{4,5},{5,4},{6,7},{7,6},{8,9},{9,8},{10,11... | collective-permute-start | bytes 491528 | tf_op jit(solution)/shard_map/ppermute | solution.py:428
  56.1 6.8 %collective-permute-start.15 = (f32[128,256]{1,0:T(8,128)S(1)}, f32[128,256]{1,0:T(8,128)S(1)}, u32[]{:S(2)}, u32[]{:S(2)}) collective-permute-start(f32[128,256]{1,0:T(8,128)S(1)} %shard_map.92.own_ref), channel_id=1, source_target_pairs={{0,32},{32,0},{64,96},{96,64},{128,160},{160,128},{192,224},{224,1... | collective-permute-start | bytes 393224 | tf_op jit(solution)/shard_map/ppermute | solution.py:428
  66.6 7.3 %collective-permute-start.18 = (f32[16,3712]{1,0:T(8,128)S(1)}, f32[16,3712]{1,0:T(8,128)S(1)}, u32[]{:S(2)}, u32[]{:S(2)}) collective-permute-start(f32[16,3712]{1,0:T(8,128)S(1)} %get-tuple-element.57), channel_id=1, source_target_pairs={{0,1},{1,0},{2,3},{3,2},{4,5},{5,4},{6,7},{7,6},{8,9},{9,8},{10,11... | collective-permute-start | bytes 712712 | tf_op jit(solution)/shard_map/ppermute | solution.py:428
  66.7 12.7 %collective-permute-start.19 = (f32[16,3712]{1,0:T(8,128)S(1)}, f32[16,3712]{1,0:T(8,128)S(1)}, u32[]{:S(2)}, u32[]{:S(2)}) collective-permute-start(f32[16,3712]{1,0:T(8,128)S(1)} %get-tuple-element.58), channel_id=1, source_target_pairs={{0,2},{1,3},{2,0},{3,1},{4,6},{5,7},{6,4},{7,5},{8,10},{9,11},{10,... | collective-permute-start | bytes 712712 | tf_op jit(solution)/shard_map/ppermute | solution.py:428
  68.5 12.9 %collective-permute-start.20 = (f32[16,3712]{1,0:T(8,128)S(1)}, f32[16,3712]{1,0:T(8,128)S(1)}, u32[]{:S(2)}, u32[]{:S(2)}) collective-permute-start(f32[16,3712]{1,0:T(8,128)S(1)} %get-tuple-element.59), channel_id=1, source_target_pairs={{0,3},{1,2},{2,1},{3,0},{4,7},{5,6},{6,5},{7,4},{8,11},{9,10},{10,... | collective-permute-start | bytes 712712 | tf_op jit(solution)/shard_map/ppermute | solution.py:428
  86.7 6.9 %collective-permute-start.22 = (f32[16,2176]{1,0:T(8,128)S(1)}, f32[16,2176]{1,0:T(8,128)S(1)}, u32[]{:S(2)}, u32[]{:S(2)}) collective-permute-start(f32[16,2176]{1,0:T(8,128)S(1)} %shard_map.99.own.gate_ref), channel_id=1, source_target_pairs={{0,8},{1,9},{2,10},{3,11},{4,12},{5,13},{6,14},{7,15},{8,0},{9,1},... | collective-permute-start | bytes 417800 | tf_op jit(solution)/shard_map/ppermute | solution.py:428
  89.4 7.1 %collective-permute-start.24 = (f32[16,1536]{1,0:T(8,128)S(1)}, f32[16,1536]{1,0:T(8,128)S(1)}, u32[]{:S(2)}, u32[]{:S(2)}) collective-permute-start(f32[16,1536]{1,0:T(8,128)S(1)} %get-tuple-element.60), channel_id=1, source_target_pairs={{0,1},{1,0},{2,3},{3,2},{4,5},{5,4},{6,7},{7,6},{8,9},{9,8},{10,11... | collective-permute-start | bytes 294920 | tf_op jit(solution)/shard_map/ppermute | solution.py:428
  89.7 6.8 %collective-permute-start.25 = (f32[16,1536]{1,0:T(8,128)S(1)}, f32[16,1536]{1,0:T(8,128)S(1)}, u32[]{:S(2)}, u32[]{:S(2)}) collective-permute-start(f32[16,1536]{1,0:T(8,128)S(1)} %get-tuple-element.61), channel_id=1, source_target_pairs={{0,2},{1,3},{2,0},{3,1},{4,6},{5,7},{6,4},{7,5},{8,10},{9,11},{10,... | collective-permute-start | bytes 294920 | tf_op jit(solution)/shard_map/ppermute | solution.py:428
  93.7 8.8 %collective-permute-start.23 = (f32[16,1664]{1,0:T(8,128)S(1)}, f32[16,1664]{1,0:T(8,128)S(1)}, u32[]{:S(2)}, u32[]{:S(2)}) collective-permute-start(f32[16,1664]{1,0:T(8,128)S(1)} %shard_map.100.own), channel_id=1, source_target_pairs={{0,24},{1,25},{2,26},{3,27},{4,28},{5,29},{6,30},{7,31},{8,16},{9,... | collective-permute-start | bytes 319496 | tf_op jit(solution)/shard_map/ppermute | solution.py:428
  97.6 13.9 %collective-permute-start.33 = (f32[64,768]{1,0:T(8,128)S(1)}, f32[64,768]{1,0:T(8,128)S(1)}, u32[]{:S(2)}, u32[]{:S(2)}) collective-permute-start(f32[64,768]{1,0:T(8,128)S(1)} %get-tuple-element.67), channel_id=1, source_target_pairs={{0,32},{32,0},{64,96},{96,64},{128,160},{160,128},{192,224},{224,1... | collective-permute-start | bytes 589832 | tf_op jit(solution)/shard_map/ppermute | solution.py:428
  108.2 6.7 %collective-permute-start.32 = (f32[16,2176]{1,0:T(8,128)S(1)}, f32[16,2176]{1,0:T(8,128)S(1)}, u32[]{:S(2)}, u32[]{:S(2)}) collective-permute-start(f32[16,2176]{1,0:T(8,128)S(1)} %shard_map.103.b0), channel_id=1, source_target_pairs={{0,3},{1,2},{2,1},{3,0},{4,7},{5,6},{6,5},{7,4},{8,11},{9,10},{10,... | collective-permute-start | bytes 417800 | tf_op jit(solution)/shard_map/ppermute | solution.py:428
  108.9 6.0 %collective-permute-start.31 = (f32[16,2176]{1,0:T(8,128)S(1)}, f32[16,2176]{1,0:T(8,128)S(1)}, u32[]{:S(2)}, u32[]{:S(2)}) collective-permute-start(f32[16,2176]{1,0:T(8,128)S(1)} %shard_map.103.b0), channel_id=1, source_target_pairs={{0,2},{1,3},{2,0},{3,1},{4,6},{5,7},{6,4},{7,5},{8,10},{9,11},{10,... | collective-permute-start | bytes 417800 | tf_op jit(solution)/shard_map/ppermute | solution.py:428
  109.1 6.3 %collective-permute-start.30 = (f32[16,2176]{1,0:T(8,128)S(1)}, f32[16,2176]{1,0:T(8,128)S(1)}, u32[]{:S(2)}, u32[]{:S(2)}) collective-permute-start(f32[16,2176]{1,0:T(8,128)S(1)} %shard_map.103.b0), channel_id=1, source_target_pairs={{0,1},{1,0},{2,3},{3,2},{4,5},{5,4},{6,7},{7,6},{8,9},{9,8},{10,11... | collective-permute-start | bytes 417800 | tf_op jit(solution)/shard_map/ppermute | solution.py:428
  115.5 6.5 %collective-permute-start.34 = (f32[64,1408]{1,0:T(8,128)S(1)}, f32[64,1408]{1,0:T(8,128)S(1)}, u32[]{:S(2)}, u32[]{:S(2)}) collective-permute-start(f32[64,1408]{1,0:T(8,128)S(1)} %get-tuple-element.69), channel_id=1, source_target_pairs={{0,32},{32,0},{64,96},{96,64},{128,160},{160,128},{192,224},{224,1... | collective-permute-start | bytes 1081352 | tf_op jit(solution)/shard_map/ppermute | solution.py:428
  (17 other events, 92.4 us)
